TPU v7x, 512 devices: a whole 4x4x16 slice. The times are simulated.
512 devices in a mesh: vocab: 32 (over x, y, core), dp: 16 (over z).
Axes of the slice: x: 4, y: 4, z: 16, core: 2. Of those that a mesh axis runs over, the one named last changes fastest.
Arguments:
- hidden: bfloat16 [2048, 2048], P('dp', 'vocab')
- head_weight: bfloat16 [2048, 65536], P('dp', 'vocab')
- teacher_logits: bfloat16 [2048, 65536], P('dp', 'vocab')
- target_ids: int32 [2048], P('dp'), may hold values from 0 to 65535
- segment_ids: int32 [16, 128], P('dp'), may hold values from 0 to 15, never falling along the last dimension, each value on 1 to 16 neighbouring positions
- pair_order: int32 [16, 16], P('dp'), may hold values from 0 to 15, each once within a row
Outputs:
- hidden_grad: bfloat16 [2048, 2048], P('dp', 'vocab')
- head_grad: float32 [2048, 65536], P('dp', 'vocab')
- loss: float32 [], replicated
Inputs may be any that keep to these rules, and one draw needn't show every extreme that they name: `segment_ids`: in each group the row's sequence number never falls along the rows, and every sequence has 1 to 16 rows. `pair_order`: each group's row is a permutation of its 16 sequences; pair p is entry 2p (chosen) and entry 2p + 1 (rejected).
All inputs are finite; a program needn't handle non-finite values.
Results may differ from a plain program's by a relative error of at most 0.018.
Values may be sent and summed in bfloat16 or wider, within the bound.
No kernel may reach another device: no remote copies, remote signals or barrier semaphores. Data moves between devices by JAX's collectives and lax.ppermute only.
A program may use at most 64 MiB of HBM per device.

v0:
```python
import jax
import jax.numpy as jnp
from jax import lax
from jax.sharding import PartitionSpec as P

dpo_beta = 0.1
dpo_gamma = 4.0


def pair_weights(log_ratio, segments, ordering):
    seq_count = ordering.shape[0]
    labels = lax.broadcasted_iota(jnp.int32, (1, seq_count), 1)
    seq_hot = (segments[:, None] == labels).astype(jnp.float32)
    seq_ratio = jnp.sum(seq_hot * log_ratio[:, None], axis=0)
    chosen = ordering[0::2]
    rejected = ordering[1::2]
    chosen_hot = (chosen[:, None] == labels).astype(jnp.float32)
    rejected_hot = (rejected[:, None] == labels).astype(jnp.float32)
    margin = dpo_beta * (
        jnp.sum(chosen_hot * seq_ratio[None, :], axis=1)
        - jnp.sum(rejected_hot * seq_ratio[None, :], axis=1)
    )
    strength = dpo_gamma * dpo_beta * jax.nn.sigmoid(-margin)
    coeffs = jnp.sum((rejected_hot - chosen_hot) * strength[:, None], axis=0)
    row_weight = jnp.sum(seq_hot * coeffs[None, :], axis=1)
    return (row_weight, jnp.sum(jax.nn.softplus(-margin)))


def on_device(hidden, head_weight, teacher_logits, target_ids, segment_ids, pair_order):
    rows_full = lax.all_gather(hidden, "vocab", axis=1, tiled=True)
    weight_full = lax.all_gather(head_weight, "dp", axis=0, tiled=True)
    student = jnp.dot(rows_full, weight_full, preferred_element_type=jnp.float32)
    teacher = teacher_logits.astype(jnp.float32)
    shard_width = student.shape[1]
    offset = lax.axis_index("vocab") * shard_width
    column = lax.broadcasted_iota(jnp.int32, student.shape, 1) + offset
    is_target = column == target_ids[:, None]
    local_target = jnp.sum(jnp.where(is_target, student, 0.0), axis=1)
    local_tgt_teach = jnp.sum(jnp.where(is_target, teacher, 0.0), axis=1)
    local_max = jnp.max(student, axis=1)
    local_tmax = jnp.max(teacher, axis=1)
    max_student, max_teacher = lax.pmax((local_max, local_tmax), "vocab")
    exp_student = jnp.exp(student - max_student[:, None])
    exp_teacher = jnp.exp(teacher - max_teacher[:, None])
    sum_student, sum_teacher, cross, target_student, target_teacher = lax.psum(
        (
            jnp.sum(exp_student, axis=1),
            jnp.sum(exp_teacher, axis=1),
            jnp.sum(exp_teacher * (teacher - student), axis=1),
            local_target,
            local_tgt_teach,
        ),
        "vocab",
    )
    lse_student = max_student + jnp.log(sum_student)
    lse_teacher = max_teacher + jnp.log(sum_teacher)
    kl_rows = cross / sum_teacher - lse_teacher + lse_student
    log_ratio = target_student - lse_student - (target_teacher - lse_teacher)
    row_weight, dpo_sum = pair_weights(log_ratio, segment_ids[0], pair_order[0])
    group_objective = jnp.sum(kl_rows) + dpo_gamma * dpo_sum
    summed_objective = lax.psum(group_objective, "dp")
    loss_value = summed_objective / (rows_full.shape[0] * lax.axis_size("dp"))
    prob_student = exp_student / sum_student[:, None]
    prob_teacher = exp_teacher / sum_teacher[:, None]
    logit_grad = (
        prob_student
        - prob_teacher
        + row_weight[:, None] * (is_target.astype(jnp.float32) - prob_student)
    ).astype(jnp.bfloat16)
    hidden_term = lax.dot_general(
        logit_grad, weight_full, (((1,), (1,)), ((), ())), preferred_element_type=jnp.float32
    )
    hidden_grad = lax.psum_scatter(
        hidden_term.astype(jnp.bfloat16), "vocab", scatter_dimension=1, tiled=True
    )
    grad_cols = lax.all_to_all(rows_full, "dp", split_axis=1, concat_axis=0, tiled=True)
    head_grad = lax.dot_general(
        grad_cols,
        lax.all_gather(logit_grad, "dp", axis=0, tiled=True),
        (((0,), (0,)), ((), ())),
        preferred_element_type=jnp.float32,
    )
    return (hidden_grad, head_grad, loss_value)


def solution(mesh):
    return jax.shard_map(
        on_device,
        mesh=mesh,
        in_specs=(
            P("dp", "vocab"),
            P("dp", "vocab"),
            P("dp", "vocab"),
            P("dp"),
            P("dp", None),
            P("dp", None),
        ),
        out_specs=(P("dp", "vocab"), P("dp", "vocab"), P()),
        check_vma=False,
    )
```

profile of v0, /device:TPU:2, one launch (start us, length us, event | category | flops | bytes accessed | tf_op | source)
XLA Modules:
  0.0 486.9 jit_solution(1537256044486397161)
XLA Ops:
  7.2 0.0 all-gather.3.cloned.1.call-start
  7.2 0.7 all-gather.3.cloned.1.call-update
  7.9 0.0 copy-start
  7.9 0.0 all-gather.5.cloned.1.call-start
  8.0 0.8 slice.7
  8.8 0.7 slice.6
  9.5 1.2 reduce_max.24
  10.7 29.9 %all_gather.9 = bf16[128,2048]{0,1:T(8,128)(2,1)} all-gather(bf16[128,64]{0,1:T(8,128)(2,1)} %param.6), channel_id=1, replica_groups=mesh['vocab'=32,'dp'=16] {'vocab'}, dimensions={1}, use_global_device_ids=true | all-gather | bytes 540672 | tf_op jit(solution)/shard_map/all_gather | solution.py:30
  40.6 79.9 %all-gather.3.cloned.1.call-done = bf16[2048,2048]{1,0:T(8,128)(2,1)} async-done(((bf16[128,2048]{1,0:T(8,128)(2,1)}), bf16[2048,2048]{1,0:T(8,128)(2,1)}) %all-gather.3.cloned.1.call-update) | async-done | bytes 8388624 | tf_op jit(solution)/shard_map/all_gather | solution.py:31
  120.5 4.9 %fusion.14 = (f32[128]{0:T(128)S(1)}, f32[128,2048]{1,0:T(8,128)S(1)}) fusion(bf16[128,2048]{0,1:T(8,128)(2,1)} %all_gather.9, bf16[2048,2048]{1,0:T(8,128)(2,1)} %all-gather.3.cloned.1.call-done), kind=kOutput, calls=%fused_computation.38 | convolution fusion | flops 1074003840 | bytes 9961984 | tf_op jit(solution)/shard_map/dot_general | solution.py:32
  125.4 56.2 %all-reduce.1 = (f32[128]{0:T(128)S(1)}, f32[128]{0:T(128)S(1)}) all-reduce(bf16[128]{0:T(256)(128)(2,1)S(1)} %reduce_max.24, f32[128]{0:T(128)S(1)} %get-tuple-element.33), channel_id=1, replica_groups=mesh['vocab'=32,'dp'=16] {'vocab'}, use_global_device_ids=true, to_apply=%region_5.6 | all-reduce | flops 256 | bytes 1792 | tf_op jit(solution)/shard_map/pmax | solution.py:42
  181.6 0.8 fusion.6
  182.4 56.8 %all-reduce = (f32[128]{0:T(128)S(1)}, f32[128]{0:T(128)S(1)}, f32[128]{0:T(128)S(1)}, f32[128]{0:T(128)S(1)}, f32[128]{0:T(128)S(1)}) all-reduce(f32[128]{0:T(128)S(1)} %get-tuple-element.18, f32[128]{0:T(128)S(1)} %get-tuple-element.16, f32[128]{0:T(128)S(1)} %get-tuple-element.19, ...), channel_id=1, replica_groups=mesh['vocab'=32,'dp'=16] {'vocab'}, use_global_device_ids=true, to_apply=%region_11.12 | all-reduce | flops 640 | bytes 5120 | tf_op jit(solution)/shard_map/psum | solution.py:45
  239.2 0.6 add_reduce_fusion
  239.9 0.1 select_reduce_fusion.1
  240.0 0.2 select_reduce_fusion.2
  240.2 0.6 fusion.13
  240.8 0.1 multiply_reduce_fusion
  240.9 0.1 select_reduce_fusion
  241.0 1.4 fusion.11
  242.4 0.0 all-gather.5.cloned.1.call-update
  242.4 8.9 %all-to-all-start = ((bf16[128,16,128]{0,2,1:T(8,128)(2,1)}), bf16[128,16,128]{0,2,1:T(8,128)(2,1)S(1)}, u32[]{:S(2)}, u32[]{:S(2)}) async-start(bf16[128,16,128]{0,2,1:T(8,128)(2,1)} %bitcast.2), calls=%async_computation.1 | async-start | bytes 1048576 | tf_op jit(solution)/shard_map/all_to_all | solution.py:76
  251.3 0.0 reduce-scatter.2.cloned.1.call-start
  251.4 6.7 %convolution_convert_fusion = bf16[128,2048]{0,1:T(8,128)(2,1)} fusion(bf16[128,2048]{1,0:T(8,128)(2,1)} %fusion.11, bf16[2048,2048]{1,0:T(8,128)(2,1)} %all-gather.3.cloned.1.call-done), kind=kOutput, calls=%fused_computation.1 | convolution fusion | flops 1074003968 | bytes 9437184 | tf_op jit(solution)/shard_map/dot_general | solution.py:70
  258.1 0.0 reduce-scatter.2.cloned.1.call-update
  259.3 21.5 %all-to-all-done = bf16[128,16,128]{0,2,1:T(8,128)(2,1)S(1)} async-done(((bf16[128,16,128]{0,2,1:T(8,128)(2,1)}), bf16[128,16,128]{0,2,1:T(8,128)(2,1)S(1)}, u32[]{:S(2)}, u32[]{:S(2)}) %all-to-all-start) | async-done | bytes 524320 | tf_op jit(solution)/shard_map/all_to_all | solution.py:76
  280.9 0.3 copy.13
  281.1 32.6 %psum.47 = f32[]{:T(128)} all-reduce(f32[]{:T(128)S(6)} %add.55), channel_id=1, replica_groups=mesh['vocab'=32,'dp'=16] {'dp'}, use_global_device_ids=true, to_apply=%region_22.23 | all-reduce | flops 1 | bytes 8 | tf_op jit(solution)/shard_map/psum | solution.py:61
  314.4 48.8 %all-gather.5.cloned.1.call-done = bf16[2048,2048]{1,0:T(8,128)(2,1)} async-done(((bf16[128,2048]{1,0:T(8,128)(2,1)}), bf16[2048,2048]{1,0:T(8,128)(2,1)}) %all-gather.5.cloned.1.call-update) | async-done | bytes 8388624 | tf_op jit(solution)/shard_map/all_gather | solution.py:79
  363.2 5.8 %convolution_bitcast_fusion = f32[128,2048]{0,1:T(8,128)S(1)} fusion(bf16[2048,2048]{1,0:T(8,128)(2,1)} %all-gather.5.cloned.1.call-done, bf16[2048,128]{1,0:T(8,128)(2,1)S(1)} %bitcast.14), kind=kOutput, calls=%fused_computation | convolution fusion | flops 1073741824 | bytes 9961472 | tf_op jit(solution)/shard_map/dot_general | solution.py:77
  369.0 1.3 copy.14
  370.3 109.0 %reduce-scatter.2.cloned.1.call-done = bf16[128,64]{0,1:T(8,128)(2,1)} async-done(((bf16[128,2048]{0,1:T(8,128)(2,1)}), bf16[128,64]{0,1:T(8,128)(2,1)}) %reduce-scatter.2.cloned.1.call-update) | async-done | bytes 16400 | tf_op jit(solution)/shard_map/reduce_scatter | solution.py:73
  (6 shorter events, 0.0 us)
Async XLA Ops:
  7.2 113.3 %all-gather.3.cloned.1.call-start = ((), (), s32[]{:S(2)}) async-start(), calls=%async_computation.2 | async-start | bytes 8912896 | tf_op jit(solution)/shard_map/all_gather | solution.py:31
  7.9 173.7 %copy-start = (bf16[128,2048]{1,0:T(8,128)(2,1)S(1)}, bf16[128,2048]{1,0:T(8,128)(2,1)}, u32[]{:S(2)}) copy-start(bf16[128,2048]{1,0:T(8,128)(2,1)} %param.8) | copy-start | bytes 1572868
  7.9 173.7 %copy-start.1 = (s32[128]{0:T(128)S(1)}, s32[128]{0:T(128)}, u32[]{:S(2)}) copy-start(s32[128]{0:T(128)} %param.9) | copy-start | bytes 1540
  7.9 355.3 %all-gather.5.cloned.1.call-start = ((), (), s32[]{:S(2)}) async-start(), calls=%async_computation.4 | async-start | bytes 8912896 | tf_op jit(solution)/shard_map/all_gather | solution.py:79
  40.6 199.2 %copy-start.2 = (s32[1,128]{1,0:T(1,128)S(1)}, s32[1,128]{1,0:T(1,128)}, u32[]{:S(2)}) copy-start(s32[1,128]{1,0:T(1,128)} %param.10) | copy-start | bytes 1540
  242.4 38.4 %all-to-all-start = ((bf16[128,16,128]{0,2,1:T(8,128)(2,1)}), bf16[128,16,128]{0,2,1:T(8,128)(2,1)S(1)}, u32[]{:S(2)}, u32[]{:S(2)}) async-start(bf16[128,16,128]{0,2,1:T(8,128)(2,1)} %bitcast.2), calls=%async_computation.1 | async-start | bytes 1048576 | tf_op jit(solution)/shard_map/all_to_all | solution.py:76
  251.3 227.9 %reduce-scatter.2.cloned.1.call-start = ((), (), s32[]{:S(2)}) async-start(), calls=%async_computation.3 | async-start | bytes 540672 | tf_op jit(solution)/shard_map/reduce_scatter | solution.py:73
Sparse Core Ops, SparseCore 0:
  10.1 110.3 all-gather.2
  242.6 120.6 all-gather.4
  368.1 111.0 reduce-scatter.1
where the time goes:
time: 487 us
  waiting for transfers between devices  260 us (53%)
  blocking collectives  175 us (36%)
  matrix products  17.4 us (4%)
  between operations  16.8 us (3%)
  starting transfers between devices  9 us (2%)
  other arithmetic  5.2 us (1%)
    reduce_scatter x1, waiting for transfers between devices, on_device(): lax.psum_scatter(hidden_term.astype(jnp.bfloat16), 'vocab', scatter_dimen...  109 us
    all_gather x1, waiting for transfers between devices, on_device(): weight_full = lax.all_gather(head_weight, 'dp', axis=0, tiled=True)  79.9 us
    psum x1, blocking collectives, on_device(): lax.psum((jnp.sum(exp_student, axis=1), jnp.sum(exp_teacher, axis=1), jnp...  56.8 us
    pmax x1, blocking collectives, on_device(): max_student, max_teacher = lax.pmax((local_max, local_tmax), 'vocab')  56.2 us
    all_gather x1, waiting for transfers between devices, on_device(): lax.all_gather(logit_grad, 'dp', axis=0, tiled=True)  48.8 us
    psum x1, blocking collectives, on_device(): summed_objective = lax.psum(group_objective, 'dp')  32.6 us
    all_gather x1, blocking collectives, on_device(): rows_full = lax.all_gather(hidden, 'vocab', axis=1, tiled=True)  29.9 us
    all_to_all x1, waiting for transfers between devices, on_device(): lax.all_to_all(rows_full, 'dp', split_axis=1, concat_axis=0, tiled=True)  21.5 us
  transfers between devices with their start and end apart: 4, of which 4 were waited for; matrix products, arithmetic and copies ran while one was open for 3% of the time, Pallas kernels for 0%

commit v1 on v0

--- a/solution.py
+++ b/solution.py
@@ -28,7 +28,10 @@
 
 def on_device(hidden, head_weight, teacher_logits, target_ids, segment_ids, pair_order):
     rows_full = lax.all_gather(hidden, "vocab", axis=1, tiled=True)
-    weight_full = lax.all_gather(head_weight, "dp", axis=0, tiled=True)
+    devices = lax.axis_size("dp")
+    parts = jnp.stack([head_weight for _ in range(devices)])
+    parts = lax.all_to_all(parts, "dp", split_axis=0, concat_axis=0)
+    weight_full = jnp.concatenate(parts, axis=0)
     student = jnp.dot(rows_full, weight_full, preferred_element_type=jnp.float32)
     teacher = teacher_logits.astype(jnp.float32)
     shard_width = student.shape[1]

time: 487 us -> 671 us (1.38)
  the two profiles are of different devices: /device:TPU:2 before, /device:TPU:1 now
where the time goes in v1:
time: 671 us; the launch traced here: 670 us
  waiting for transfers between devices  405 us (60%)
  blocking collectives  190 us (28%)
  starting transfers between devices  27.3 us (4%)
  between operations  18.5 us (3%)
  matrix products  17.6 us (3%)
  local copies, waits for them, and re-layouts  7.12 us (1%)
    all_to_all x1, waiting for transfers between devices, on_device(): parts = lax.all_to_all(parts, 'dp', split_axis=0, concat_axis=0)  333 us
    psum x1, blocking collectives, on_device(): lax.psum((jnp.sum(exp_student, axis=1), jnp.sum(exp_teacher, axis=1), jnp...  66.3 us
    pmax x1, blocking collectives, on_device(): max_student, max_teacher = lax.pmax((local_max, local_tmax), 'vocab')  64.7 us
    all_gather x1, waiting for transfers between devices, on_device(): lax.all_gather(logit_grad, 'dp', axis=0, tiled=True)  50.9 us
    psum x1, blocking collectives, on_device(): summed_objective = lax.psum(group_objective, 'dp')  31.1 us
    all_gather x1, blocking collectives, on_device(): rows_full = lax.all_gather(hidden, 'vocab', axis=1, tiled=True)  28.1 us
    all_to_all x1, waiting for transfers between devices, on_device(): lax.all_to_all(rows_full, 'dp', split_axis=1, concat_axis=0, tiled=True)  21.3 us
    all_to_all x1, starting transfers between devices, on_device(): parts = lax.all_to_all(parts, 'dp', split_axis=0, concat_axis=0)  15.9 us
  transfers between devices with their start and end apart: 4, of which 3 were waited for; matrix products, arithmetic and copies ran while one was open for 2% of the time, Pallas kernels for 0%

profile of v1, /device:TPU:1, one launch (start us, length us, event | category | flops | bytes accessed | tf_op | source)
XLA Modules:
  0.0 670.2 jit_solution(5568163110719790844)
XLA Ops:
  8.0 5.3 stack.2
  13.3 15.9 %all-to-all-start = ((bf16[16,128,2048]{2,1,0:T(8,128)(2,1)}), bf16[16,128,2048]{2,1,0:T(8,128)(2,1)}, u32[]{:S(2)}, u32[]{:S(2)}) async-start(bf16[16,128,2048]{2,1,0:T(8,128)(2,1)} %stack.2), calls=%async_computation | async-start | bytes 16777216 | tf_op jit(solution)/shard_map/all_to_all | solution.py:33
  29.3 0.0 copy-start.2
  29.3 0.0 all-gather.2.cloned.1.call-start
  29.3 0.1 slice.6
  29.4 0.1 slice.7
  29.5 0.0 copy-done
  29.5 0.2 reduce_max.24
  29.7 28.1 %all_gather.6 = bf16[128,2048]{0,1:T(8,128)(2,1)} all-gather(bf16[128,64]{0,1:T(8,128)(2,1)S(1)} %copy-done.1), channel_id=1, replica_groups=mesh['vocab'=32,'dp'=16] {'vocab'}, dimensions={1}, use_global_device_ids=true | all-gather | bytes 540672 | tf_op jit(solution)/shard_map/all_gather | solution.py:30
  57.8 333.0 %all-to-all-done = bf16[16,128,2048]{2,1,0:T(8,128)(2,1)} async-done(((bf16[16,128,2048]{2,1,0:T(8,128)(2,1)}), bf16[16,128,2048]{2,1,0:T(8,128)(2,1)}, u32[]{:S(2)}, u32[]{:S(2)}) %all-to-all-start) | async-done | bytes 8388640 | tf_op jit(solution)/shard_map/all_to_all | solution.py:33
  390.8 4.9 fusion.14
  395.7 64.7 %all-reduce.1 = (f32[128]{0:T(128)S(1)}, f32[128]{0:T(128)S(1)}) all-reduce(bf16[128]{0:T(256)(128)(2,1)S(1)} %reduce_max.24, f32[128]{0:T(128)S(1)} %get-tuple-element.33), channel_id=1, replica_groups=mesh['vocab'=32,'dp'=16] {'vocab'}, use_global_device_ids=true, to_apply=%region_5.6 | all-reduce | flops 256 | bytes 1792 | tf_op jit(solution)/shard_map/pmax | solution.py:45
  460.5 0.8 fusion.6
  461.3 66.3 %all-reduce = (f32[128]{0:T(128)S(1)}, f32[128]{0:T(128)S(1)}, f32[128]{0:T(128)S(1)}, f32[128]{0:T(128)S(1)}, f32[128]{0:T(128)S(1)}) all-reduce(f32[128]{0:T(128)S(1)} %get-tuple-element.18, f32[128]{0:T(128)S(1)} %get-tuple-element.16, f32[128]{0:T(128)S(1)} %get-tuple-element.19, ...), channel_id=1, replica_groups=mesh['vocab'=32,'dp'=16] {'vocab'}, use_global_device_ids=true, to_apply=%region_11.12 | all-reduce | flops 640 | bytes 5120 | tf_op jit(solution)/shard_map/psum | solution.py:48
  527.6 0.6 add_reduce_fusion
  528.2 0.1 select_reduce_fusion.1
  528.3 0.2 select_reduce_fusion.2
  528.5 0.6 fusion.13
  529.2 0.1 multiply_reduce_fusion
  529.3 0.1 select_reduce_fusion
  529.4 1.4 fusion.11
  530.8 0.0 all-gather.2.cloned.1.call-update
  530.8 11.3 %all-to-all-start.1 = ((bf16[128,16,128]{0,2,1:T(8,128)(2,1)}), bf16[128,16,128]{0,2,1:T(8,128)(2,1)S(1)}, u32[]{:S(2)}, u32[]{:S(2)}) async-start(bf16[128,16,128]{0,2,1:T(8,128)(2,1)} %bitcast.3), calls=%async_computation.2 | async-start | bytes 1048576 | tf_op jit(solution)/shard_map/all_to_all | solution.py:79
  542.1 0.0 reduce-scatter.2.cloned.1.call-start
  542.2 6.9 %convolution_convert_fusion = bf16[128,2048]{0,1:T(8,128)(2,1)} fusion(bf16[128,2048]{1,0:T(8,128)(2,1)} %fusion.11, bf16[2048,2048]{1,0:T(8,128)(2,1)} %bitcast), kind=kOutput, calls=%fused_computation.1 | convolution fusion | flops 1074003968 | bytes 9437184 | tf_op jit(solution)/shard_map/dot_general | solution.py:73
  549.1 0.0 reduce-scatter.2.cloned.1.call-update
  550.3 21.3 %all-to-all-done.1 = bf16[128,16,128]{0,2,1:T(8,128)(2,1)S(1)} async-done(((bf16[128,16,128]{0,2,1:T(8,128)(2,1)}), bf16[128,16,128]{0,2,1:T(8,128)(2,1)S(1)}, u32[]{:S(2)}, u32[]{:S(2)}) %all-to-all-start.1) | async-done | bytes 524320 | tf_op jit(solution)/shard_map/all_to_all | solution.py:79
  571.6 0.3 copy.13
  571.9 31.1 %psum.47 = f32[]{:T(128)} all-reduce(f32[]{:T(128)S(6)} %add.55), channel_id=1, replica_groups=mesh['vocab'=32,'dp'=16] {'dp'}, use_global_device_ids=true, to_apply=%region_22.23 | all-reduce | flops 1 | bytes 8 | tf_op jit(solution)/shard_map/psum | solution.py:64
  603.7 50.9 %all-gather.2.cloned.1.call-done = bf16[2048,2048]{1,0:T(8,128)(2,1)} async-done(((bf16[128,2048]{1,0:T(8,128)(2,1)}), bf16[2048,2048]{1,0:T(8,128)(2,1)}) %all-gather.2.cloned.1.call-update) | async-done | bytes 8388624 | tf_op jit(solution)/shard_map/all_gather | solution.py:82
  654.5 5.8 convolution_bitcast_fusion
  660.3 1.3 copy.14
  (10 shorter events, 0.0 us)
Async XLA Ops:
  13.3 16.0 %copy-start.3 = (s32[1,16]{1,0:T(1,128)S(1)}, s32[1,16]{1,0:T(1,128)}, u32[]{:S(2)}) copy-start(s32[1,16]{1,0:T(1,128)} %param.11) | copy-start | bytes 196
  13.3 16.2 %copy-start = (bf16[128,2048]{1,0:T(8,128)(2,1)S(1)}, bf16[128,2048]{1,0:T(8,128)(2,1)}, u32[]{:S(2)}) copy-start(bf16[128,2048]{1,0:T(8,128)(2,1)} %param.8) | copy-start | bytes 1572868
  13.3 16.4 %copy-start.1 = (bf16[128,64]{0,1:T(8,128)(2,1)S(1)}, bf16[128,64]{0,1:T(8,128)(2,1)}, u32[]{:S(2)}) copy-start(bf16[128,64]{0,1:T(8,128)(2,1)} %param.6) | copy-start | bytes 49156
  13.3 377.5 %all-to-all-start = ((bf16[16,128,2048]{2,1,0:T(8,128)(2,1)}), bf16[16,128,2048]{2,1,0:T(8,128)(2,1)}, u32[]{:S(2)}, u32[]{:S(2)}) async-start(bf16[16,128,2048]{2,1,0:T(8,128)(2,1)} %stack.2), calls=%async_computation | async-start | bytes 16777216 | tf_op jit(solution)/shard_map/all_to_all | solution.py:33
  29.3 431.2 %copy-start.2 = (s32[128]{0:T(128)S(1)}, s32[128]{0:T(128)}, u32[]{:S(2)}) copy-start(s32[128]{0:T(128)} %param.9) | copy-start | bytes 1540
  29.3 625.2 %all-gather.2.cloned.1.call-start = ((), (), s32[]{:S(2)}) async-start(), calls=%async_computation.4 | async-start | bytes 8912896 | tf_op jit(solution)/shard_map/all_gather | solution.py:82
  390.8 137.4 %copy-start.4 = (s32[1,128]{1,0:T(1,128)S(1)}, s32[1,128]{1,0:T(1,128)}, u32[]{:S(2)}) copy-start(s32[1,128]{1,0:T(1,128)} %param.10) | copy-start | bytes 1540
  530.8 40.8 %all-to-all-start.1 = ((bf16[128,16,128]{0,2,1:T(8,128)(2,1)}), bf16[128,16,128]{0,2,1:T(8,128)(2,1)S(1)}, u32[]{:S(2)}, u32[]{:S(2)}) async-start(bf16[128,16,128]{0,2,1:T(8,128)(2,1)} %bitcast.3), calls=%async_computation.2 | async-start | bytes 1048576 | tf_op jit(solution)/shard_map/all_to_all | solution.py:79
  542.1 119.4 %reduce-scatter.2.cloned.1.call-start = ((), (), s32[]{:S(2)}) async-start(), calls=%async_computation.3 | async-start | bytes 540672 | tf_op jit(solution)/shard_map/reduce_scatter | solution.py:76
Sparse Core Ops, SparseCore 0:
  530.9 123.5 all-gather.1
Sparse Core Ops, SparseCore 1:
  549.2 95.1 reduce-scatter.1
